TPU v7x, 32 devices: a whole 2x2x4 slice. The times are simulated.
32 devices in a mesh: pipe: 2 (over y), lat: 4 (over x, core), lon: 4 (over z).
Axes of the slice: x: 2, y: 2, z: 4, core: 2. Of those that a mesh axis runs over, the one named last changes fastest.
Arguments:
- field: bfloat16 [192, 64, 1024], P(None, 'lat', 'lon'), may hold values from -6 to 6
- conv_weight: bfloat16 [192, 1728], replicated, may hold values from -0.15625 to 0.15625
- conv_bias: float32 [192], replicated, may hold values from -3 to 3
- expand_weight: bfloat16 [768, 192], replicated, may hold values from -0.4375 to 0.4375
- expand_bias: float32 [768], replicated, may hold values from -3 to 3
- project_weight: bfloat16 [192, 768], replicated, may hold values from -0.21875 to 0.21875
- project_bias: float32 [192], replicated, may hold values from -3 to 3
- out_cotangent: bfloat16 [192, 32, 512], P(None, 'lat', 'lon'), may hold values from -6 to 6
- dropout_key: int32 [2], replicated, may hold values from 0 to 1073741823
Outputs:
- section_fields: bfloat16 [2, 192, 32, 512], P('pipe', None, 'lat', 'lon')
- conv_grad: float32 [192, 1728], replicated
- conv_bias_grad: float32 [192], replicated
- expand_grad: float32 [768, 192], replicated
- expand_bias_grad: float32 [768], replicated
- project_grad: float32 [192, 768], replicated
- project_bias_grad: float32 [192], replicated
All inputs are finite; a program needn't handle non-finite values.
Results may differ from a plain program's by a relative error of at most 0.0056.
Values may be sent and summed in bfloat16 or wider, within the bound.
A program may use at most 64 MiB of HBM per device.

v0:
```python
import jax
import jax.numpy as jnp
from jax import lax
from jax.sharding import PartitionSpec as P

MIXER_ONE = -2048144789
MIXER_TWO = -1028477387
GOLDEN_STEP = -1640531535
KEEP_LEVEL = 819
KEEP_SCALE = 1024.0 / 819.0


def passed_along(value, axis, steps):
    count = lax.axis_size(axis)
    pairs = [(source, (source + steps) % count) for source in range(count)]
    return lax.ppermute(value, axis, pairs)


def shifted_2(block, axis, distance):
    devices = range(lax.axis_size(axis))
    route = [(i - distance, i) for i in devices if i - distance in devices]
    return lax.ppermute(block, axis, route)


def shifted(number, places):
    return lax.shift_right_logical(number, jnp.full_like(number, places))


def scramble(number):
    number = number ^ shifted(number, 16)
    number = number * jnp.int32(MIXER_ONE)
    number = number ^ shifted(number, 13)
    number = number * jnp.int32(MIXER_TWO)
    return number ^ shifted(number, 16)


def keep_mask(cell_index, dropout_key):
    salt = scramble(dropout_key[0] + scramble(dropout_key[1]))
    hashed = scramble(cell_index * jnp.int32(GOLDEN_STEP) + salt)
    bucket = jnp.bitwise_and(shifted(hashed, 8), jnp.int32(1023))
    return jnp.where(bucket < KEEP_LEVEL, jnp.float32(KEEP_SCALE), jnp.float32(0.0))


def gelu_slope(point, incoming):
    return jax.vjp(jax.nn.gelu, point)[1](incoming)[0]


def outer_sum(left, right):
    return lax.dot_general(
        left, right, (((1,), (1,)), ((), ())), preferred_element_type=jnp.float32
    )


def contract_first(weight, right):
    return lax.dot_general(
        weight, right, (((0,), (0,)), ((), ())), preferred_element_type=jnp.float32
    )


def parity_planes(padded, out_rows, out_cols):
    channels = padded.shape[0]
    even_sized = jnp.pad(padded, ((0, 0), (0, 1), (0, 1)))
    split = even_sized.reshape(channels, out_rows + 1, 2, out_cols + 1, 2)
    return jnp.transpose(split, (2, 4, 0, 1, 3))


def tap_slice(planes, tap_row, tap_col, out_rows, out_cols):
    plane = planes[tap_row % 2, tap_col % 2]
    channels = plane.shape[0]
    row_from = tap_row // 2
    col_from = tap_col // 2
    piece = lax.slice(
        plane, (0, row_from, col_from), (channels, row_from + out_rows, col_from + out_cols)
    )
    return piece.reshape(channels, out_rows * out_cols)


def convolve(conv_weight, planes, out_rows, out_cols):
    channels = planes.shape[2]
    total = None
    for tap_row in range(3):
        for tap_col in range(3):
            tap = 3 * tap_row + tap_col
            term = jnp.dot(
                conv_weight[:, tap * channels : (tap + 1) * channels],
                tap_slice(planes, tap_row, tap_col, out_rows, out_cols),
                preferred_element_type=jnp.float32,
            )
            total = term if total is None else total + term
    return total


def kernel_gradient(d_half, planes, out_rows, out_cols):
    blocks = []
    for tap_row in range(3):
        for tap_col in range(3):
            blocks.append(
                outer_sum(d_half, tap_slice(planes, tap_row, tap_col, out_rows, out_cols))
            )
    return jnp.concatenate(blocks, axis=1)


def hand_over(payload):
    return passed_along(payload, "pipe", 1)


def per_device(
    field,
    conv_weight,
    conv_bias,
    expand_weight,
    expand_bias,
    project_weight,
    project_bias,
    out_cotangent,
    dropout_key,
):
    channels, row_count, col_count = field.shape
    hidden_count = expand_weight.shape[0]
    half_rows = row_count // 2
    half_cols = col_count // 2
    lat_count = lax.axis_size("lat")
    lon_count = lax.axis_size("lon")
    scale = float(half_rows * lat_count * half_cols * lon_count) ** (-0.5)
    pipe_index = lax.axis_index("pipe")
    is_encoder = pipe_index == 0
    from_above = shifted_2(field[:, row_count - 1 :, :], "lat", 1)
    mirrored = passed_along(field[:, :1, :], "lon", lon_count // 2)
    top_row = jnp.where(lax.axis_index("lat") == 0, mirrored, from_above)
    extended = jnp.concatenate([top_row, field], axis=1)
    west_edge = passed_along(extended[:, :, col_count - 1 :], "lon", 1)
    padded = jnp.concatenate([west_edge, extended], axis=2)
    row_start = 0
    cell_count = half_rows * half_cols
    planes = parity_planes(padded, half_rows, half_cols)
    row_ids = lax.axis_index("lat") * half_rows + row_start + jnp.arange(half_rows, dtype=jnp.int32)
    col_ids = lax.axis_index("lon") * half_cols + jnp.arange(half_cols, dtype=jnp.int32)
    cell_ids = (row_ids[:, None] * (half_cols * lon_count) + col_ids[None, :]).reshape(-1)
    keep = keep_mask(cell_ids, dropout_key)[None, :]

    def encode():
        pre = convolve(conv_weight, planes, half_rows, half_cols) + conv_bias[:, None]
        encoded = (jax.nn.gelu(pre) * keep).astype(jnp.bfloat16)
        return (encoded, pre)

    def encode_empty():
        return (
            jnp.zeros((channels, cell_count), jnp.bfloat16),
            jnp.zeros((channels, cell_count), jnp.float32),
        )

    def process(received):
        inner = (
            jnp.dot(expand_weight, received, preferred_element_type=jnp.float32)
            + expand_bias[:, None]
        )
        activated = jax.nn.gelu(inner).astype(jnp.bfloat16)
        processed = (
            received.astype(jnp.float32)
            + jnp.dot(project_weight, activated, preferred_element_type=jnp.float32)
            + project_bias[:, None]
        ).astype(jnp.bfloat16)
        scaled = out_cotangent.reshape(channels, cell_count).astype(jnp.float32) * scale
        cot_half = scaled.astype(jnp.bfloat16)
        project_grad = outer_sum(cot_half, activated)
        d_inner = gelu_slope(inner, contract_first(project_weight, cot_half))
        d_inner_half = d_inner.astype(jnp.bfloat16)
        expand_grad = outer_sum(d_inner_half, received)
        d_encoded = (scaled + contract_first(expand_weight, d_inner_half)).astype(jnp.bfloat16)
        flat = jnp.concatenate(
            [
                expand_grad.reshape(-1),
                jnp.sum(d_inner, axis=1),
                project_grad.reshape(-1),
                jnp.sum(scaled, axis=1),
            ]
        )
        return (processed, d_encoded, flat)

    enc_len = conv_weight.size + channels
    proc_len = 2 * expand_weight.size + hidden_count + channels

    def process_empty():
        return (
            jnp.zeros((channels, cell_count), jnp.bfloat16),
            jnp.zeros((channels, cell_count), jnp.bfloat16),
            jnp.zeros((proc_len,), jnp.float32),
        )

    def backward(pre_now, d_encoded_now):
        d_pre = gelu_slope(pre_now, d_encoded_now.astype(jnp.float32) * keep)
        conv_grad = kernel_gradient(d_pre.astype(jnp.bfloat16), planes, half_rows, half_cols)
        return jnp.concatenate([conv_grad.reshape(-1), jnp.sum(d_pre, axis=1)])

    def backward_empty():
        return jnp.zeros((enc_len,), jnp.float32)

    encoded, pre_saved = lax.cond(is_encoder, encode, encode_empty)
    received = hand_over(encoded)
    processed, d_encoded, flat_proc = lax.cond(is_encoder, process_empty, lambda: process(received))
    returned = hand_over(d_encoded)
    flat_enc = lax.cond(is_encoder, lambda: backward(pre_saved, returned), backward_empty)
    section_fields = jnp.where(is_encoder, encoded, processed).reshape(
        1, channels, half_rows, half_cols
    )
    combined = jnp.concatenate([flat_enc, flat_proc])
    total = lax.psum(combined, ("pipe", "lat", "lon"))
    enc_total = total[:enc_len]
    proc_total = total[enc_len:]
    weight_count = conv_weight.size
    conv_grad = enc_total[:weight_count].reshape(conv_weight.shape)
    conv_bias_grad = enc_total[weight_count:]
    expand_count = expand_weight.size
    expand_grad = proc_total[:expand_count].reshape(expand_weight.shape)
    expand_bias_grad = proc_total[expand_count : expand_count + hidden_count]
    project_start = expand_count + hidden_count
    project_grad = proc_total[project_start : project_start + expand_count].reshape(
        project_weight.shape
    )
    project_bias_grad = proc_total[project_start + expand_count :]
    return (
        section_fields,
        conv_grad,
        conv_bias_grad,
        expand_grad,
        expand_bias_grad,
        project_grad,
        project_bias_grad,
    )


def solution(mesh):
    placed = (P(None, "lat", "lon"), P(), P(), P(), P(), P(), P(), P(None, "lat", "lon"), P())
    return jax.shard_map(
        per_device,
        mesh=mesh,
        in_specs=placed,
        out_specs=(P("pipe", None, "lat", "lon"), P(), P(), P(), P(), P(), P()),
        check_vma=False,
    )
```

profile of v0, /device:TPU:0, one launch (start us, length us, event | category | flops | bytes accessed | tf_op | source)
XLA Modules:
  0.0 278.3 jit_solution(14114148621795843833)
XLA Ops:
  7.2 1.7 fusion.114
  8.9 4.1 %collective-permute-start = (bf16[192,1,256]{2,0,1:T(8,128)(2,1)S(1)}, bf16[192,1,256]{2,0,1:T(8,128)(2,1)S(1)}, u32[]{:S(2)}, u32[]{:S(2)}) collective-permute-start(bf16[192,1,256]{2,0,1:T(8,128)(2,1)S(1)} %copy.47), channel_id=1, source_target_pairs={{0,2},{1,3},{2,0},{3,1},{4,6},{5,7},{6,4},{7,5},{8,10},{9,11},{10,... | collective-permute-start | bytes 294920 | tf_op jit(solution)/shard_map/ppermute | solution.py:16
  13.0 1.5 collective-permute-start.1
  14.5 1.3 fusion.115
  17.9 3.6 %copy.37 = bf16[192,16,256]{0,1,2:T(8,128)(2,1)S(1)} copy(bf16[192,16,256]{2,1,0:T(8,128)(2,1)} %param.15) | data formatting | bytes 3145728 | tf_op args[0]
  21.8 1.6 collective-permute-start.2
  23.4 3.9 %collective-permute-done.2 = bf16[192,17,1]{0,1,2:T(8,128)(2,1)S(1)} collective-permute-done((bf16[192,17,1]{0,1,2:T(8,128)(2,1)S(1)}, bf16[192,17,1]{0,1,2:T(8,128)(2,1)S(1)}, u32[]{:S(2)}, u32[]{:S(2)}) %collective-permute-start.2) | collective-permute-done | bytes 6560 | tf_op jit(solution)/shard_map/ppermute | solution.py:16
  27.3 2.7 fusion.97
  30.0 6.4 %reshape.189 = bf16[192,9,2,129,2]{0,2,1,4,3:T(2,128)(2,1)} reshape(bf16[192,18,258]{0,1,2:T(8,128)(2,1)} %fusion.97) | data formatting | bytes 3566592 | tf_op jit(solution)/shard_map/reshape | solution.py:63
  36.4 3.5 %copy.150 = bf16[192,9,2,129,2]{0,4,3,2,1:T(2,128)(2,1)S(1)} copy(bf16[192,9,2,129,2]{0,2,1,4,3:T(2,128)(2,1)} %reshape.189) | data formatting | bytes 3566592 | tf_op jit(solution)/shard_map/reshape | solution.py:63
  40.0 19.9 %conditional.3 = ((bf16[192,1024]{1,0:T(8,128)(2,1)}, f32[192,1024]{1,0:T(8,128)S(1)})) conditional(s32[]{:T(128)} %convert_element_type.39, () %tuple.30, (bf16[192,1728]{1,0:T(8,128)(2,1)}, bf16[2,2,192,9,129]{2,1,4,0,3:T(2,128)(2,1)S(1)}, f32[192]{0:T(256)S(1)}, f32[1,1024]{1,0:T(1,128)S(1)}) %tuple.92), branch_computations={%region_0.1_spmd, %region_1.2_spmd} | conditional | flops 683212800 | bytes 35056676 | solution.py:198
  40.0 11.7 %copy.39 = bf16[2,2,192,9,129]{4,3,2,1,0:T(8,128)(2,1)} copy(bf16[2,2,192,9,129]{2,1,4,0,3:T(2,128)(2,1)S(1)} %get-tuple-element.104) | data formatting | bytes 3566592 | tf_op jit(solution)/shard_map
  51.7 3.2 %slice_bitcast_fusion = (bf16[192,9,129]{2,1,0:T(8,128)(2,1)S(1)}, bf16[192,9,129]{2,1,0:T(8,128)(2,1)S(1)}, bf16[192,9,129]{2,1,0:T(8,128)(2,1)S(1)}, bf16[192,9,129]{2,1,0:T(8,128)(2,1)S(1)}) fusion(bf16[2,2,192,9,129]{4,3,2,1,0:T(8,128)(2,1)} %copy.39), kind=kLoop, calls=%fused_computation | loop fusion | bytes 3566592 | tf_op jit(solution)/shard_map/cond/branch_1_fun/squeeze | solution.py:68
  58.6 1.2 fusion.9
  59.9 12.1 %collective-permute-done.3 = bf16[192,1024]{1,0:T(8,128)(2,1)S(1)} collective-permute-done((bf16[192,1024]{1,0:T(8,128)(2,1)}, bf16[192,1024]{1,0:T(8,128)(2,1)S(1)}, u32[]{:S(2)}, u32[]{:S(2)}) %collective-permute-start.3) | collective-permute-done | bytes 393248 | tf_op jit(solution)/shard_map/ppermute | solution.py:16
  72.4 19.1 %collective-permute-start.4 = (bf16[192,1024]{1,0:T(8,128)(2,1)S(1)}, bf16[192,1024]{1,0:T(8,128)(2,1)}, u32[]{:S(2)}, u32[]{:S(2)}) collective-permute-start(bf16[192,1024]{1,0:T(8,128)(2,1)S(1)} %get-tuple-element.59), channel_id=1, source_target_pairs={{0,16},{16,0},{1,17},{17,1},{2,18},{18,2},{3,19},{19,3},{4,20},{20... | collective-permute-start | bytes 1179656 | tf_op jit(solution)/shard_map/ppermute | solution.py:16
  91.5 9.5 %collective-permute-done.4 = bf16[192,1024]{1,0:T(8,128)(2,1)} collective-permute-done((bf16[192,1024]{1,0:T(8,128)(2,1)S(1)}, bf16[192,1024]{1,0:T(8,128)(2,1)}, u32[]{:S(2)}, u32[]{:S(2)}) %collective-permute-start.4) | collective-permute-done | bytes 393248 | tf_op jit(solution)/shard_map/ppermute | solution.py:16
  101.1 25.0 %conditional.5 = (f32[331968]{0:T(1024)S(1)}) conditional(s32[]{:T(128)} %convert_element_type.39, () %tuple.34, (bf16[192,1024]{1,0:T(8,128)(2,1)}, f32[1,1024]{1,0:T(1,128)S(1)}, f32[192,1024]{1,0:T(8,128)}, bf16[2,2,192,9,129]{2,1,4,0,3:T(2,128)(2,1)S(1)}) %tuple.88), branch_computations={%region_6.7_spmd, %region_7.9_spmd} | conditional | flops 684331008 | bytes 36876584 | solution.py:202
  101.1 11.7 %copy.41 = bf16[2,2,192,9,129]{4,3,2,1,0:T(8,128)(2,1)} copy(bf16[2,2,192,9,129]{2,1,4,0,3:T(2,128)(2,1)S(1)} %get-tuple-element.116) | data formatting | bytes 3566592 | tf_op jit(solution)/shard_map
  112.7 3.2 %slice_bitcast_fusion.4 = (bf16[192,9,129]{2,1,0:T(8,128)(2,1)S(1)}, bf16[192,9,129]{2,1,0:T(8,128)(2,1)S(1)}, bf16[192,9,129]{2,1,0:T(8,128)(2,1)S(1)}, bf16[192,9,129]{2,1,0:T(8,128)(2,1)S(1)}) fusion(bf16[2,2,192,9,129]{4,3,2,1,0:T(8,128)(2,1)} %copy.41), kind=kLoop, calls=%fused_computation.80 | loop fusion | bytes 3566592 | tf_op jit(solution)/shard_map/cond/branch_1_fun/squeeze | solution.py:68
  117.1 1.6 fusion.103
  120.7 1.0 fusion.72
  121.6 1.0 fusion.78
  123.6 1.4 concatenate.13
  126.0 3.2 %pad_maximum_fusion.2 = f32[627840]{0:T(1024)} fusion(f32[295872]{0:T(1024)} %copy-done.4, f32[331968]{0:T(1024)S(1)} %get-tuple-element.183), kind=kLoop, calls=%fused_computation.131 | loop fusion | flops 627840 | bytes 5022720 | tf_op jit(solution)/shard_map/concatenate | solution.py:206
  131.2 129.0 %all-reduce.3.cloned.1.call-done = f32[627840]{0:T(1024)} async-done(((f32[627840]{0:T(1024)}), f32[627840]{0:T(1024)}) %all-reduce.3.cloned.1.call-update) | async-done | bytes 2511376 | tf_op jit(solution)/shard_map/psum | solution.py:207
  260.2 1.3 slice-done
  261.5 1.5 reshape.186
  263.0 2.6 fusion.113
  265.7 1.4 reshape.187
  267.1 1.1 copy.42
  268.1 2.0 reshape.188
  (71 shorter events, 12.7 us)
Async XLA Ops:
  7.2 253.0 %all-reduce.3.cloned.1.call-start = ((), (), s32[]{:S(2)}) async-start(), calls=%async_computation | async-start | bytes 5029888 | tf_op jit(solution)/shard_map/psum | solution.py:207
  8.9 12.6 %collective-permute-start = (bf16[192,1,256]{2,0,1:T(8,128)(2,1)S(1)}, bf16[192,1,256]{2,0,1:T(8,128)(2,1)S(1)}, u32[]{:S(2)}, u32[]{:S(2)}) collective-permute-start(bf16[192,1,256]{2,0,1:T(8,128)(2,1)S(1)} %copy.47), channel_id=1, source_target_pairs={{0,2},{1,3},{2,0},{3,1},{4,6},{5,7},{6,4},{7,5},{8,10},{9,11},{10,... | collective-permute-start | bytes 294920 | tf_op jit(solution)/shard_map/ppermute | solution.py:16
  13.0 8.5 %collective-permute-start.1 = (bf16[192,1,256]{2,0,1:T(8,128)(2,1)S(1)}, bf16[192,1,256]{2,0,1:T(8,128)(2,1)S(1)}, u32[]{:S(2)}, u32[]{:S(2)}) collective-permute-start(bf16[192,1,256]{2,0,1:T(8,128)(2,1)S(1)} %copy.48), channel_id=1, source_target_pairs={{0,4},{4,8},{8,12},{1,5},{5,9},{9,13},{2,6},{6,10},{10,14},{3,7},{... | collective-permute-start | bytes 294920 | tf_op jit(solution)/shard_map/ppermute | solution.py:22
  21.8 5.5 %collective-permute-start.2 = (bf16[192,17,1]{0,1,2:T(8,128)(2,1)S(1)}, bf16[192,17,1]{0,1,2:T(8,128)(2,1)S(1)}, u32[]{:S(2)}, u32[]{:S(2)}) collective-permute-start(bf16[192,17,1]{0,1,2:T(8,128)(2,1)S(1)} %pad_maximum_fusion.3), channel_id=1, source_target_pairs={{0,1},{1,2},{2,3},{3,0},{4,5},{5,6},{6,7},{7,4},{8,9},{9,10},{10,1... | collective-permute-start | bytes 19592 | tf_op jit(solution)/shard_map/ppermute | solution.py:16
  36.4 3.5 %copy-start.19 = (f32[192]{0:T(256)S(1)}, f32[192]{0:T(256)}, u32[]{:S(2)}) copy-start(f32[192]{0:T(256)} %param.17) | copy-start | bytes 2308
  40.0 32.0 %copy-start.14 = (bf16[768,192]{0,1:T(8,128)(2,1)S(1)}, bf16[768,192]{0,1:T(8,128)(2,1)}, u32[]{:S(2)}) copy-start(bf16[768,192]{0,1:T(8,128)(2,1)} %param.18) | copy-start | bytes 884740
  40.0 32.0 %copy-start.17 = (f32[192]{0:T(256)S(1)}, f32[192]{0:T(256)}, u32[]{:S(2)}) copy-start(f32[192]{0:T(256)} %param.21) | copy-start | bytes 2308
  40.0 32.0 %copy-start.18 = (f32[768]{0:T(1024)S(1)}, f32[768]{0:T(1024)}, u32[]{:S(2)}) copy-start(f32[768]{0:T(1024)} %param.19) | copy-start | bytes 9220
  55.0 1.1 copy-start.12
  59.9 12.1 %copy-start.5 = (f32[192,1024]{1,0:T(8,128)}, f32[192,1024]{1,0:T(8,128)S(1)}, u32[]{:S(2)}) copy-start(f32[192,1024]{1,0:T(8,128)S(1)} %get-tuple-element.60) | copy-start | bytes 2359300
  59.9 12.1 %collective-permute-start.3 = (bf16[192,1024]{1,0:T(8,128)(2,1)}, bf16[192,1024]{1,0:T(8,128)(2,1)S(1)}, u32[]{:S(2)}, u32[]{:S(2)}) collective-permute-start(bf16[192,1024]{1,0:T(8,128)(2,1)} %get-tuple-element.57), channel_id=1, source_target_pairs={{0,16},{16,0},{1,17},{17,1},{2,18},{18,2},{3,19},{19,3},{4,20},{20... | collective-permute-start | bytes 1179656 | tf_op jit(solution)/shard_map/ppermute | solution.py:16
  72.4 28.6 %copy-start.4 = (f32[295872]{0:T(1024)}, f32[295872]{0:T(1024)S(1)}, u32[]{:S(2)}) copy-start(f32[295872]{0:T(1024)S(1)} %get-tuple-element.61) | copy-start | bytes 3550468
  72.4 28.6 %copy-start.7 = (bf16[192,1024]{1,0:T(8,128)(2,1)}, bf16[192,1024]{1,0:T(8,128)(2,1)S(1)}, u32[]{:S(2)}) copy-start(bf16[192,1024]{1,0:T(8,128)(2,1)S(1)} %get-tuple-element.58) | copy-start | bytes 1179652
  72.4 28.6 %collective-permute-start.4 = (bf16[192,1024]{1,0:T(8,128)(2,1)S(1)}, bf16[192,1024]{1,0:T(8,128)(2,1)}, u32[]{:S(2)}, u32[]{:S(2)}) collective-permute-start(bf16[192,1024]{1,0:T(8,128)(2,1)S(1)} %get-tuple-element.59), channel_id=1, source_target_pairs={{0,16},{16,0},{1,17},{17,1},{2,18},{18,2},{3,19},{19,3},{4,20},{20... | collective-permute-start | bytes 1179656 | tf_op jit(solution)/shard_map/ppermute | solution.py:16
  116.0 1.1 copy-start.6
  129.2 1.0 copy-start.8
  129.2 1.1 copy-start.9
  260.2 1.3 slice-start
  265.7 4.5 %copy-start.3 = (f32[627840]{0:T(1024)S(1)}, f32[627840]{0:T(1024)}, u32[]{:S(2)}) copy-start(f32[627840]{0:T(1024)} %all-reduce.3.cloned.1.call-done) | copy-start | bytes 7534084
Sparse Core Ops, SparseCore 0:
  129.4 130.8 all-reduce.2
where the time goes:
time: 279 us; the launch traced here: 278 us
  waiting for transfers between devices  155 us (56%)
  local copies, waits for them, and re-layouts  64.8 us (23%)
  starting transfers between devices  26.4 us (9%)
  between operations  16.2 us (6%)
  matrix products  8.09 us (3%)
  other arithmetic  7.87 us (3%)
    psum x1, waiting for transfers between devices, per_device(): total = lax.psum(combined, ('pipe', 'lat', 'lon'))  129 us
    ppermute x4, waiting for transfers between devices, passed_along(): return lax.ppermute(value, axis, pairs)  25.5 us
    ppermute x4, starting transfers between devices, passed_along(): return lax.ppermute(value, axis, pairs)  24.9 us
    another operation x5, local copies, waits for them, and re-layouts  23.6 us
    reshape x2, local copies, waits for them, and re-layouts, parity_planes(): split = even_sized.reshape(channels, out_rows + 1, 2, out_cols + 1, 2)  9.93 us
    unnamed x25, local copies, waits for them, and re-layouts  6.66 us
    squeeze x2, local copies, waits for them, and re-layouts, tap_slice(): plane = planes[tap_row % 2, tap_col % 2]  6.47 us
  transfers between devices with their start and end apart: 6, of which 4 were waited for; matrix products, arithmetic and copies ran while one was open for 2% of the time, Pallas kernels for 0%

commit v1 on v0

--- a/solution.py
+++ b/solution.py
@@ -1,13 +1,23 @@
+import functools
 import jax
 import jax.numpy as jnp
 from jax import lax
 from jax.sharding import PartitionSpec as P
+from jax.lax import psum
 
 MIXER_ONE = -2048144789
 MIXER_TWO = -1028477387
 GOLDEN_STEP = -1640531535
 KEEP_LEVEL = 819
 KEEP_SCALE = 1024.0 / 819.0
+
+
+def list_frame(z_in, device_axis, bus_axis):
+    clean = psum(z_in, device_axis)
+    return psum(clean, bus_axis)
+
+
+show_cells_up = functools.partial(list_frame, device_axis=("lat", "lon"), bus_axis="pipe")
 
 
 def passed_along(value, axis, steps):
@@ -204,7 +214,7 @@
         1, channels, half_rows, half_cols
     )
     combined = jnp.concatenate([flat_enc, flat_proc])
-    total = lax.psum(combined, ("pipe", "lat", "lon"))
+    total = show_cells_up(combined)
     enc_total = total[:enc_len]
     proc_total = total[enc_len:]
     weight_count = conv_weight.size

time: 279 us -> 318 us (1.14)
  waiting for transfers between devices: 155 us -> 194 us
    psum x1 -> x2, waiting for transfers between devices: 129 us -> 169 us  [the longest x1 96.1 us: list_frame(): clean = psum(z_in, device_axis)]
  transfers between devices with their start and end apart: 6 -> 7, of which waited for: 4 -> 5; matrix products, arithmetic and copies ran while one was open for 2% -> 2% of each run, Pallas kernels for 0% -> 0%
where the time goes in v1:
time: 318 us; the launch traced here: 317 us
  waiting for transfers between devices  194 us (61%)
  local copies, waits for them, and re-layouts  63.7 us (20%)
  starting transfers between devices  26.4 us (8%)
  between operations  16.2 us (5%)
  matrix products  8.09 us (3%)
  other arithmetic  7.82 us (2%)
    psum x1, waiting for transfers between devices, list_frame(): clean = psum(z_in, device_axis)  96.1 us
    psum x1, waiting for transfers between devices, list_frame(): return psum(clean, bus_axis)  72.8 us
    ppermute x4, waiting for transfers between devices, passed_along(): return lax.ppermute(value, axis, pairs)  25.5 us
    ppermute x4, starting transfers between devices, passed_along(): return lax.ppermute(value, axis, pairs)  24.9 us
    another operation x5, local copies, waits for them, and re-layouts  23.6 us
    reshape x2, local copies, waits for them, and re-layouts, parity_planes(): split = even_sized.reshape(channels, out_rows + 1, 2, out_cols + 1, 2)  9.93 us
    squeeze x2, local copies, waits for them, and re-layouts, tap_slice(): plane = planes[tap_row % 2, tap_col % 2]  6.47 us
  transfers between devices with their start and end apart: 7, of which 5 were waited for; matrix products, arithmetic and copies ran while one was open for 2% of the time, Pallas kernels for 0%

profile of v1, /device:TPU:0, one launch (start us, length us, event | category | flops | bytes accessed | tf_op | source)
XLA Modules:
  0.0 317.1 jit_solution(7849952106211091627)
XLA Ops:
  7.2 1.7 fusion.114
  8.9 4.1 %collective-permute-start = (bf16[192,1,256]{2,0,1:T(8,128)(2,1)S(1)}, bf16[192,1,256]{2,0,1:T(8,128)(2,1)S(1)}, u32[]{:S(2)}, u32[]{:S(2)}) collective-permute-start(bf16[192,1,256]{2,0,1:T(8,128)(2,1)S(1)} %copy.47), channel_id=1, source_target_pairs={{0,2},{1,3},{2,0},{3,1},{4,6},{5,7},{6,4},{7,5},{8,10},{9,11},{10,... | collective-permute-start | bytes 294920 | tf_op jit(solution)/shard_map/ppermute | solution.py:26
  13.0 1.5 collective-permute-start.1
  14.5 1.3 fusion.115
  17.9 3.6 %copy.37 = bf16[192,16,256]{0,1,2:T(8,128)(2,1)S(1)} copy(bf16[192,16,256]{2,1,0:T(8,128)(2,1)} %param.15) | data formatting | bytes 3145728 | tf_op args[0]
  21.8 1.6 collective-permute-start.2
  23.4 3.9 %collective-permute-done.2 = bf16[192,17,1]{0,1,2:T(8,128)(2,1)S(1)} collective-permute-done((bf16[192,17,1]{0,1,2:T(8,128)(2,1)S(1)}, bf16[192,17,1]{0,1,2:T(8,128)(2,1)S(1)}, u32[]{:S(2)}, u32[]{:S(2)}) %collective-permute-start.2) | collective-permute-done | bytes 6560 | tf_op jit(solution)/shard_map/ppermute | solution.py:26
  27.3 2.7 fusion.97
  30.0 6.4 %reshape.189 = bf16[192,9,2,129,2]{0,2,1,4,3:T(2,128)(2,1)} reshape(bf16[192,18,258]{0,1,2:T(8,128)(2,1)} %fusion.97) | data formatting | bytes 3566592 | tf_op jit(solution)/shard_map/reshape | solution.py:73
  36.4 3.5 %copy.150 = bf16[192,9,2,129,2]{0,4,3,2,1:T(2,128)(2,1)S(1)} copy(bf16[192,9,2,129,2]{0,2,1,4,3:T(2,128)(2,1)} %reshape.189) | data formatting | bytes 3566592 | tf_op jit(solution)/shard_map/reshape | solution.py:73
  40.0 19.9 %conditional.3 = ((bf16[192,1024]{1,0:T(8,128)(2,1)}, f32[192,1024]{1,0:T(8,128)S(1)})) conditional(s32[]{:T(128)} %convert_element_type.39, () %tuple.30, (bf16[192,1728]{1,0:T(8,128)(2,1)}, bf16[2,2,192,9,129]{2,1,4,0,3:T(2,128)(2,1)S(1)}, f32[192]{0:T(256)S(1)}, f32[1,1024]{1,0:T(1,128)S(1)}) %tuple.94), branch_computations={%region_0.1_spmd, %region_1.2_spmd} | conditional | flops 683212800 | bytes 35056676 | solution.py:208
  40.0 11.7 %copy.39 = bf16[2,2,192,9,129]{4,3,2,1,0:T(8,128)(2,1)} copy(bf16[2,2,192,9,129]{2,1,4,0,3:T(2,128)(2,1)S(1)} %get-tuple-element.104) | data formatting | bytes 3566592 | tf_op jit(solution)/shard_map
  51.7 3.2 %slice_bitcast_fusion = (bf16[192,9,129]{2,1,0:T(8,128)(2,1)S(1)}, bf16[192,9,129]{2,1,0:T(8,128)(2,1)S(1)}, bf16[192,9,129]{2,1,0:T(8,128)(2,1)S(1)}, bf16[192,9,129]{2,1,0:T(8,128)(2,1)S(1)}) fusion(bf16[2,2,192,9,129]{4,3,2,1,0:T(8,128)(2,1)} %copy.39), kind=kLoop, calls=%fused_computation | loop fusion | bytes 3566592 | tf_op jit(solution)/shard_map/cond/branch_1_fun/squeeze | solution.py:78
  58.6 1.2 fusion.9
  59.9 12.1 %collective-permute-done.3 = bf16[192,1024]{1,0:T(8,128)(2,1)S(1)} collective-permute-done((bf16[192,1024]{1,0:T(8,128)(2,1)}, bf16[192,1024]{1,0:T(8,128)(2,1)S(1)}, u32[]{:S(2)}, u32[]{:S(2)}) %collective-permute-start.3) | collective-permute-done | bytes 393248 | tf_op jit(solution)/shard_map/ppermute | solution.py:26
  72.4 19.1 %collective-permute-start.4 = (bf16[192,1024]{1,0:T(8,128)(2,1)S(1)}, bf16[192,1024]{1,0:T(8,128)(2,1)}, u32[]{:S(2)}, u32[]{:S(2)}) collective-permute-start(bf16[192,1024]{1,0:T(8,128)(2,1)S(1)} %get-tuple-element.59), channel_id=1, source_target_pairs={{0,16},{16,0},{1,17},{17,1},{2,18},{18,2},{3,19},{19,3},{4,20},{20... | collective-permute-start | bytes 1179656 | tf_op jit(solution)/shard_map/ppermute | solution.py:26
  91.5 9.5 %collective-permute-done.4 = bf16[192,1024]{1,0:T(8,128)(2,1)} collective-permute-done((bf16[192,1024]{1,0:T(8,128)(2,1)S(1)}, bf16[192,1024]{1,0:T(8,128)(2,1)}, u32[]{:S(2)}, u32[]{:S(2)}) %collective-permute-start.4) | collective-permute-done | bytes 393248 | tf_op jit(solution)/shard_map/ppermute | solution.py:26
  101.1 25.0 %conditional.5 = (f32[331968]{0:T(1024)S(1)}) conditional(s32[]{:T(128)} %convert_element_type.39, () %tuple.34, (bf16[192,1024]{1,0:T(8,128)(2,1)}, f32[1,1024]{1,0:T(1,128)S(1)}, f32[192,1024]{1,0:T(8,128)}, bf16[2,2,192,9,129]{2,1,4,0,3:T(2,128)(2,1)S(1)}) %tuple.90), branch_computations={%region_6.7_spmd, %region_7.9_spmd} | conditional | flops 684331008 | bytes 36876584 | solution.py:212
  101.1 11.7 %copy.41 = bf16[2,2,192,9,129]{4,3,2,1,0:T(8,128)(2,1)} copy(bf16[2,2,192,9,129]{2,1,4,0,3:T(2,128)(2,1)S(1)} %get-tuple-element.116) | data formatting | bytes 3566592 | tf_op jit(solution)/shard_map
  112.7 3.2 %slice_bitcast_fusion.4 = (bf16[192,9,129]{2,1,0:T(8,128)(2,1)S(1)}, bf16[192,9,129]{2,1,0:T(8,128)(2,1)S(1)}, bf16[192,9,129]{2,1,0:T(8,128)(2,1)S(1)}, bf16[192,9,129]{2,1,0:T(8,128)(2,1)S(1)}) fusion(bf16[2,2,192,9,129]{4,3,2,1,0:T(8,128)(2,1)} %copy.41), kind=kLoop, calls=%fused_computation.80 | loop fusion | bytes 3566592 | tf_op jit(solution)/shard_map/cond/branch_1_fun/squeeze | solution.py:78
  117.1 1.6 fusion.103
  120.7 1.0 fusion.72
  123.6 1.4 concatenate.13
  126.0 3.1 pad_maximum_fusion.2
  129.2 96.1 %all-reduce.4.cloned.1.call-done = f32[627840]{0:T(1024)} async-done(((f32[627840]{0:T(1024)}), f32[627840]{0:T(1024)}) %all-reduce.4.cloned.1.call-update) | async-done | bytes 2511376 | tf_op jit(solution)/shard_map/psum | solution.py:16
  226.2 72.8 %all-reduce.6.cloned.1.call-done = f32[627840]{0:T(1024)} async-done(((f32[627840]{0:T(1024)}), f32[627840]{0:T(1024)}) %all-reduce.6.cloned.1.call-update) | async-done | bytes 2511376 | tf_op jit(solution)/shard_map/psum | solution.py:17
  299.1 1.3 slice-done
  300.4 1.5 reshape.186
  301.9 2.6 fusion.113
  304.5 1.4 reshape.187
  305.9 1.1 copy.42
  307.0 2.0 reshape.188
  (74 shorter events, 12.7 us)
Async XLA Ops:
  7.2 218.1 %all-reduce.4.cloned.1.call-start = ((), (), s32[]{:S(2)}) async-start(), calls=%async_computation | async-start | bytes 5029888 | tf_op jit(solution)/shard_map/psum | solution.py:16
  8.9 12.6 %collective-permute-start = (bf16[192,1,256]{2,0,1:T(8,128)(2,1)S(1)}, bf16[192,1,256]{2,0,1:T(8,128)(2,1)S(1)}, u32[]{:S(2)}, u32[]{:S(2)}) collective-permute-start(bf16[192,1,256]{2,0,1:T(8,128)(2,1)S(1)} %copy.47), channel_id=1, source_target_pairs={{0,2},{1,3},{2,0},{3,1},{4,6},{5,7},{6,4},{7,5},{8,10},{9,11},{10,... | collective-permute-start | bytes 294920 | tf_op jit(solution)/shard_map/ppermute | solution.py:26
  13.0 8.5 %collective-permute-start.1 = (bf16[192,1,256]{2,0,1:T(8,128)(2,1)S(1)}, bf16[192,1,256]{2,0,1:T(8,128)(2,1)S(1)}, u32[]{:S(2)}, u32[]{:S(2)}) collective-permute-start(bf16[192,1,256]{2,0,1:T(8,128)(2,1)S(1)} %copy.48), channel_id=1, source_target_pairs={{0,4},{4,8},{8,12},{1,5},{5,9},{9,13},{2,6},{6,10},{10,14},{3,7},{... | collective-permute-start | bytes 294920 | tf_op jit(solution)/shard_map/ppermute | solution.py:32
  21.8 5.5 %collective-permute-start.2 = (bf16[192,17,1]{0,1,2:T(8,128)(2,1)S(1)}, bf16[192,17,1]{0,1,2:T(8,128)(2,1)S(1)}, u32[]{:S(2)}, u32[]{:S(2)}) collective-permute-start(bf16[192,17,1]{0,1,2:T(8,128)(2,1)S(1)} %pad_maximum_fusion.3), channel_id=1, source_target_pairs={{0,1},{1,2},{2,3},{3,0},{4,5},{5,6},{6,7},{7,4},{8,9},{9,10},{10,1... | collective-permute-start | bytes 19592 | tf_op jit(solution)/shard_map/ppermute | solution.py:26
  36.4 3.5 %copy-start.19 = (f32[192]{0:T(256)S(1)}, f32[192]{0:T(256)}, u32[]{:S(2)}) copy-start(f32[192]{0:T(256)} %param.17) | copy-start | bytes 2308
  40.0 32.0 %copy-start.14 = (bf16[768,192]{0,1:T(8,128)(2,1)S(1)}, bf16[768,192]{0,1:T(8,128)(2,1)}, u32[]{:S(2)}) copy-start(bf16[768,192]{0,1:T(8,128)(2,1)} %param.18) | copy-start | bytes 884740
  40.0 32.0 %copy-start.17 = (f32[192]{0:T(256)S(1)}, f32[192]{0:T(256)}, u32[]{:S(2)}) copy-start(f32[192]{0:T(256)} %param.21) | copy-start | bytes 2308
  40.0 32.0 %copy-start.18 = (f32[768]{0:T(1024)S(1)}, f32[768]{0:T(1024)}, u32[]{:S(2)}) copy-start(f32[768]{0:T(1024)} %param.19) | copy-start | bytes 9220
  55.0 1.1 copy-start.12
  59.9 12.1 %copy-start.5 = (f32[192,1024]{1,0:T(8,128)}, f32[192,1024]{1,0:T(8,128)S(1)}, u32[]{:S(2)}) copy-start(f32[192,1024]{1,0:T(8,128)S(1)} %get-tuple-element.60) | copy-start | bytes 2359300
  59.9 12.1 %collective-permute-start.3 = (bf16[192,1024]{1,0:T(8,128)(2,1)}, bf16[192,1024]{1,0:T(8,128)(2,1)S(1)}, u32[]{:S(2)}, u32[]{:S(2)}) collective-permute-start(bf16[192,1024]{1,0:T(8,128)(2,1)} %get-tuple-element.57), channel_id=1, source_target_pairs={{0,16},{16,0},{1,17},{17,1},{2,18},{18,2},{3,19},{19,3},{4,20},{20... | collective-permute-start | bytes 1179656 | tf_op jit(solution)/shard_map/ppermute | solution.py:26
  72.4 28.6 %copy-start.4 = (f32[295872]{0:T(1024)}, f32[295872]{0:T(1024)S(1)}, u32[]{:S(2)}) copy-start(f32[295872]{0:T(1024)S(1)} %get-tuple-element.61) | copy-start | bytes 3550468
  72.4 28.6 %copy-start.7 = (bf16[192,1024]{1,0:T(8,128)(2,1)}, bf16[192,1024]{1,0:T(8,128)(2,1)S(1)}, u32[]{:S(2)}) copy-start(bf16[192,1024]{1,0:T(8,128)(2,1)S(1)} %get-tuple-element.58) | copy-start | bytes 1179652
  72.4 28.6 %collective-permute-start.4 = (bf16[192,1024]{1,0:T(8,128)(2,1)S(1)}, bf16[192,1024]{1,0:T(8,128)(2,1)}, u32[]{:S(2)}, u32[]{:S(2)}) collective-permute-start(bf16[192,1024]{1,0:T(8,128)(2,1)S(1)} %get-tuple-element.59), channel_id=1, source_target_pairs={{0,16},{16,0},{1,17},{17,1},{2,18},{18,2},{3,19},{19,3},{4,20},{20... | collective-permute-start | bytes 1179656 | tf_op jit(solution)/shard_map/ppermute | solution.py:26
  116.0 1.1 copy-start.6
  129.2 96.2 %copy-start.8 = (bf16[192,1024]{1,0:T(8,128)(2,1)S(1)}, bf16[192,1024]{1,0:T(8,128)(2,1)}, u32[]{:S(2)}) copy-start(bf16[192,1024]{1,0:T(8,128)(2,1)} %copy-done.7) | copy-start | bytes 1179652
  129.2 96.2 %copy-start.9 = (bf16[192,1024]{1,0:T(8,128)(2,1)S(1)}, bf16[192,1024]{1,0:T(8,128)(2,1)}, u32[]{:S(2)}) copy-start(bf16[192,1024]{1,0:T(8,128)(2,1)} %get-tuple-element.57) | copy-start | bytes 1179652
  129.2 169.9 %all-reduce.6.cloned.1.call-start = ((), (), s32[]{:S(2)}) async-start(), calls=%async_computation.1 | async-start | bytes 5029888 | tf_op jit(solution)/shard_map/psum | solution.py:17
  299.1 1.3 slice-start
  304.5 4.5 %copy-start.3 = (f32[627840]{0:T(1024)S(1)}, f32[627840]{0:T(1024)}, u32[]{:S(2)}) copy-start(f32[627840]{0:T(1024)} %all-reduce.6.cloned.1.call-done) | copy-start | bytes 7534084
Sparse Core Ops, SparseCore 0:
  129.3 95.9 all-reduce.3
  227.6 71.4 all-reduce.5
